TPU v7x, 512 devices: a whole 4x8x8 slice. The times are simulated.
512 devices in a mesh: seg: 128 (over y, x, z_lo, core), det: 4 (over z_hi).
Axes of the slice: x: 4, y: 8, z: 8 (z_hi: 4, z_lo: 2; z = z_hi * 2 + z_lo), core: 2. Of those that a mesh axis runs over, the one named last changes fastest.
Arguments:
- strain: bfloat16 [4, 128, 2, 16, 128], P('det', 'seg'), may hold values from -6 to 6
- bank: bfloat16 [512, 16, 2, 16, 128], P('seg'), as said below
- bank_list: int32 [128, 6], replicated, may hold values from 0 to 511, as said below
- block_len: int32 [512], replicated, may hold values from 1 to 16, 4352 in all
- band_edges: int32 [7], replicated, may hold values from 129 to 1919, as said below
Outputs:
- net_stat: float32 [4, 128, 96, 32, 128], P('det', 'seg')
Inputs may be any that keep to these rules, and one draw needn't show every extreme that they name: Each row of bank_list names 6 different blocks, all stored by the 8 owners with index s, s + 1, ..., s + 8 - 1 modulo 128 for segment s; at most 2 of them are stored by one owner, and exactly 2 by some owner in every row. `band_edges`: strictly rising; every band holds more than 128 bins. `bank`: entries independent, with scales that vary from template to template and from bin to bin.
All inputs are finite; a program needn't handle non-finite values.
Results may differ from a plain program's by a relative error of at most 0.0031.
Values may be sent and summed in bfloat16 or wider, within the bound.
A program may use at most 64 MiB of HBM per device.

v0:
```python
import math

import jax
import jax.numpy as jnp
from jax import lax
from jax.sharding import PartitionSpec as P

REACH = 8


epsilon = 1e-06
highest = lax.Precision.HIGHEST


def passed_along(value, axis, by):
    size = lax.axis_size(axis)
    return lax.ppermute(value, axis, [(i, (i + by) % size) for i in range(size)])


def swapped(value, axis, distance):
    mask = 2**distance
    pairs = [(source, source ^ mask) for source in range(lax.axis_size(axis))]
    return lax.ppermute(value, axis, pairs)


def turn_table(row_count, col_count, period):
    row_idx = jnp.arange(row_count, dtype=jnp.int32)[:, None]
    col_idx = jnp.arange(col_count, dtype=jnp.int32)[None, :]
    angles = 2.0 * math.pi / period * (row_idx * col_idx % period).astype(jnp.float32)
    return (jnp.cos(angles), jnp.sin(angles))


def complex_table(row_count, col_count, period):
    cosine, sine_part = turn_table(row_count, col_count, period)
    from_real = jnp.stack([cosine, sine_part], axis=1)
    from_imag = jnp.stack([-sine_part, cosine], axis=1)
    return jnp.stack([from_real, from_imag], axis=0)


def locate(block_ids, seg_idx, seg_count, blk_dev):
    owner_seg = block_ids // blk_dev
    return ((owner_seg - seg_idx) % seg_count, block_ids % blk_dev)


def place_rows(chosen, candidate, wanted):
    return jnp.where(wanted[:, None, None, None, None], candidate, chosen)


def body(strain, bank, bank_list, block_len, band_edges):
    seg_count = lax.axis_size("seg")
    own_seg = lax.axis_index("seg")
    blk_dev, blk_len, _, half_rows, row_bins = bank.shape
    assign_count = bank_list.shape[1]
    time_rows = 2 * half_rows
    time_len = time_rows * row_bins
    band_count = band_edges.shape[0] + 1
    my_list = lax.dynamic_index_in_dim(bank_list, own_seg, 0, keepdims=False)
    offsets, local_id = locate(my_list, own_seg, seg_count, blk_dev)
    chosen = jnp.zeros((assign_count,) + bank.shape[1:], bank.dtype)
    chosen = place_rows(chosen, bank[local_id], offsets == 0)
    moving = bank
    for distance in range(1, REACH):
        moving = passed_along(moving, "seg", -1)
        chosen = place_rows(chosen, moving[local_id], offsets == distance)
    lengths = block_len[my_list]
    live_mask = (jnp.arange(blk_len)[None, :] < lengths[:, None]).astype(jnp.float32).reshape(-1)
    slot_count = assign_count * blk_len
    group_size = math.gcd(slot_count, 4)
    templates = chosen.reshape(slot_count // group_size, group_size, 2, half_rows, row_bins)
    bin_index = (
        jnp.arange(half_rows, dtype=jnp.int32)[:, None] * row_bins
        + jnp.arange(row_bins, dtype=jnp.int32)[None, :]
    )
    band_of = jnp.sum(
        (bin_index[:, :, None] >= band_edges[None, None, :]).astype(jnp.int32), axis=2
    )
    band_mask = (band_of[None] == jnp.arange(band_count, dtype=jnp.int32)[:, None, None]).astype(
        jnp.float32
    )
    section_one = complex_table(half_rows, time_rows, time_rows)
    twist_cos, twist_sin = turn_table(time_rows, row_bins, time_len)
    section_two = complex_table(row_bins, row_bins, row_bins)
    strain_spec = strain[0, 0].astype(jnp.float32)
    data_re = strain_spec[0]
    data_im = strain_spec[1]

    def spectra(tmpl_re, tmpl_im, source_re, source_im):
        cross_re = source_re * tmpl_re + source_im * tmpl_im
        cross_im = source_im * tmpl_re - source_re * tmpl_im
        return jnp.stack([cross_re, cross_im], axis=1)

    def correlate_with():

        def correlate(tmpl_group):
            tmpl_spec = tmpl_group.astype(jnp.float32)
            tmpl_re = tmpl_spec[:, 0]
            tmpl_im = tmpl_spec[:, 1]
            tmpl_power = tmpl_re * tmpl_re + tmpl_im * tmpl_im
            band_power = (
                jnp.einsum("nhk,bhk->nb", tmpl_power, band_mask, precision=highest) + epsilon
            )
            total_power = jnp.sum(band_power, axis=1)
            band_share = band_power / total_power[:, None]
            inv_norm = lax.rsqrt(total_power)
            cross_spec = spectra(tmpl_re, tmpl_im, data_re, data_im)
            banded = cross_spec[:, None] * band_mask[None, :, None]
            section_out = jnp.einsum("nbchk,chdt->nbdtk", banded, section_one, precision=highest)
            first_re = section_out[:, :, 0]
            first_im = section_out[:, :, 1]
            turned = jnp.stack(
                [
                    first_re * twist_cos - first_im * twist_sin,
                    first_re * twist_sin + first_im * twist_cos,
                ],
                axis=2,
            )
            second = jnp.einsum("nbdtk,dkeu->nbetu", turned, section_two, precision=highest)
            second = second * inv_norm[:, None, None, None, None]
            snr_rows = jnp.sum(second, axis=1)
            residue = second - band_share[:, :, None, None, None] * snr_rows[:, None]
            chi_square = jnp.sum(
                jnp.sum(residue * residue, axis=2) / band_share[:, :, None, None], axis=1
            )
            return (snr_rows, chi_square)

        return correlate

    snr_rows, chi_square = lax.map(correlate_with(), templates)
    snr_rows = snr_rows.reshape(slot_count, 2, time_rows, row_bins)
    outgoing = snr_rows.astype(jnp.bfloat16)
    partner = swapped(outgoing, "det", 1).astype(jnp.float32)
    chi_square = chi_square.reshape(slot_count, time_rows, row_bins)
    joined = snr_rows + partner
    coherent = 0.5 * jnp.sum(joined * joined, axis=1)
    statistic = coherent / (1.0 + chi_square / (2.0 * (band_count - 1))) * live_mask[:, None, None]
    return statistic[None, None]


def solution(mesh):
    return jax.shard_map(
        body,
        mesh=mesh,
        in_specs=(
            P("det", "seg", None, None, None),
            P("seg", None, None, None, None),
            P(),
            P(),
            P(),
        ),
        out_specs=P("det", "seg", None, None, None),
        check_vma=False,
    )
```

profile of v0, /device:TPU:129, one launch (start us, length us, event | category | flops | bytes accessed | tf_op | source)
XLA Modules:
  0.0 309.1 jit_solution(17704061538454854957)
XLA Ops:
  0.0 2.7 collective-permute-start
  2.7 9.0 %collective-permute-done = bf16[4,16,2,16,128]{4,3,2,1,0:T(8,128)(2,1)S(1)} collective-permute-done((bf16[4,16,2,16,128]{4,3,2,1,0:T(8,128)(2,1)}, bf16[4,16,2,16,128]{4,3,2,1,0:T(8,128)(2,1)S(1)}, u32[]{:S(2)}, u32[]{:S(2)}) %collective-permute-start) | collective-permute-done | bytes 524320 | tf_op jit(solution)/shard_map/ppermute | solution.py:17
  11.8 6.8 %collective-permute-start.1 = (bf16[4,16,2,16,128]{4,3,2,1,0:T(8,128)(2,1)S(1)}, bf16[4,16,2,16,128]{4,3,2,1,0:T(8,128)(2,1)S(1)}, u32[]{:S(2)}, u32[]{:S(2)}) collective-permute-start(bf16[4,16,2,16,128]{4,3,2,1,0:T(8,128)(2,1)S(1)} %collective-permute-done), channel_id=1, source_target_pairs={{0,508},{4,0},{8,4},{12,8},{16,12},{20,16},{24,20},{28,24},{32,28}... | collective-permute-start | bytes 1572872 | tf_op jit(solution)/shard_map/ppermute | solution.py:17
  18.5 3.7 %collective-permute-done.1 = bf16[4,16,2,16,128]{4,3,2,1,0:T(8,128)(2,1)S(1)} collective-permute-done((bf16[4,16,2,16,128]{4,3,2,1,0:T(8,128)(2,1)S(1)}, bf16[4,16,2,16,128]{4,3,2,1,0:T(8,128)(2,1)S(1)}, u32[]{:S(2)}, u32[]{:S(2)}) %collective-permute-start.1) | collective-permute-done | bytes 524320 | tf_op jit(solution)/shard_map/ppermute | solution.py:17
  22.2 10.9 %collective-permute-start.2 = (bf16[4,16,2,16,128]{4,3,2,1,0:T(8,128)(2,1)S(1)}, bf16[4,16,2,16,128]{4,3,2,1,0:T(8,128)(2,1)}, u32[]{:S(2)}, u32[]{:S(2)}) collective-permute-start(bf16[4,16,2,16,128]{4,3,2,1,0:T(8,128)(2,1)S(1)} %collective-permute-done.1), channel_id=1, source_target_pairs={{0,508},{4,0},{8,4},{12,8},{16,12},{20,16},{24,20},{28,24},{32,28}... | collective-permute-start | bytes 1572872 | tf_op jit(solution)/shard_map/ppermute | solution.py:17
  33.3 1.4 collective-permute-done.2
  34.8 13.1 %collective-permute-start.3 = (bf16[4,16,2,16,128]{4,3,2,1,0:T(8,128)(2,1)}, bf16[4,16,2,16,128]{4,3,2,1,0:T(8,128)(2,1)}, u32[]{:S(2)}, u32[]{:S(2)}) collective-permute-start(bf16[4,16,2,16,128]{4,3,2,1,0:T(8,128)(2,1)} %collective-permute-done.2), channel_id=1, source_target_pairs={{0,508},{4,0},{8,4},{12,8},{16,12},{20,16},{24,20},{28,24},{32,28}... | collective-permute-start | bytes 1572872 | tf_op jit(solution)/shard_map/ppermute | solution.py:17
  50.0 13.0 %collective-permute-start.4 = (bf16[4,16,2,16,128]{4,3,2,1,0:T(8,128)(2,1)}, bf16[4,16,2,16,128]{4,3,2,1,0:T(8,128)(2,1)}, u32[]{:S(2)}, u32[]{:S(2)}) collective-permute-start(bf16[4,16,2,16,128]{4,3,2,1,0:T(8,128)(2,1)} %collective-permute-done.3), channel_id=1, source_target_pairs={{0,508},{4,0},{8,4},{12,8},{16,12},{20,16},{24,20},{28,24},{32,28}... | collective-permute-start | bytes 1572872 | tf_op jit(solution)/shard_map/ppermute | solution.py:17
  63.0 2.6 gather_fusion.7
  65.8 12.2 %collective-permute-start.5 = (bf16[4,16,2,16,128]{4,3,2,1,0:T(8,128)(2,1)}, bf16[4,16,2,16,128]{4,3,2,1,0:T(8,128)(2,1)}, u32[]{:S(2)}, u32[]{:S(2)}) collective-permute-start(bf16[4,16,2,16,128]{4,3,2,1,0:T(8,128)(2,1)} %collective-permute-done.4), channel_id=1, source_target_pairs={{0,508},{4,0},{8,4},{12,8},{16,12},{20,16},{24,20},{28,24},{32,28}... | collective-permute-start | bytes 1572872 | tf_op jit(solution)/shard_map/ppermute | solution.py:17
  78.7 1.2 collective-permute-done.5
  79.9 13.2 %collective-permute-start.6 = (bf16[4,16,2,16,128]{4,3,2,1,0:T(8,128)(2,1)}, bf16[4,16,2,16,128]{4,3,2,1,0:T(8,128)(2,1)}, u32[]{:S(2)}, u32[]{:S(2)}) collective-permute-start(bf16[4,16,2,16,128]{4,3,2,1,0:T(8,128)(2,1)} %collective-permute-done.5), channel_id=1, source_target_pairs={{0,508},{4,0},{8,4},{12,8},{16,12},{20,16},{24,20},{28,24},{32,28}... | collective-permute-start | bytes 1572872 | tf_op jit(solution)/shard_map/ppermute | solution.py:17
  93.1 2.6 gather_fusion.6
  95.7 2.6 gather_fusion.5
  98.3 2.6 gather_fusion.4
  100.9 2.6 gather_fusion.3
  103.5 2.6 gather_fusion.2
  106.1 2.6 gather_fusion.1
  108.7 2.6 gather_fusion
  111.3 3.8 %select_select_fusion = bf16[24,4,2,16,128]{4,3,2,1,0:T(8,128)(2,1)} fusion(bf16[24,4,2,16,128]{4,3,2,1,0:T(8,128)(2,1)} %bitcast.131, bf16[24,4,2,16,128]{4,3,2,1,0:T(8,128)(2,1)} %bitcast.130, bf16[24,4,2,16,128]{4,3,2,1,0:T(8,128)(2,1)} %bitcast.129, bf16[24,4,2,16,128]{4,3,2,1,0:T(8,128)(2,1)} %bitcast.128, bf16[24,4,2,16,128]{4,3,2,1,0:T(8,128)(2,1)} %bitcast.127, ...), kind=kLoop, calls=%fused_computation.67 | loop fusion | flops 3145728 | bytes 7078080 | tf_op jit(solution)/shard_map/jit(_where)/select_n | solution.py:46
  115.1 111.7 %while.14 = (s32[]{:T(128)}, f32[24,4,2,32,128]{4,3,2,1,0:T(8,128)S(1)}, f32[24,4,32,128]{3,2,1,0:T(8,128)}, f32[1,16,128]{2,1,0:T(8,128)S(1)}, bf16[24,4,2,16,1...) while((s32[]{:T(128)}, ...), condition=%wide.region_6.7_spmd.clone.clone, body=%wide.region_1.6_spmd.clone.clone.sunk | while | flops 909820032 | bytes 9380681 | solution.py:128
  153.8 1.0 convolution_bitcast_fusion.4
  167.8 1.0 convolution_bitcast_fusion.4
  181.8 1.0 convolution_bitcast_fusion.4
  195.8 1.0 convolution_bitcast_fusion.4
  209.7 1.0 convolution_bitcast_fusion.4
  226.9 1.5 bitcast_convert_fusion
  228.4 7.9 %collective-permute-start.7 = (bf16[96,2,32,128]{3,2,1,0:T(8,128)(2,1)}, bf16[96,2,32,128]{3,2,1,0:T(8,128)(2,1)}, u32[]{:S(2)}, u32[]{:S(2)}) collective-permute-start(bf16[96,2,32,128]{3,2,1,0:T(8,128)(2,1)} %bitcast_convert_fusion), channel_id=1, source_target_pairs={{0,2},{1,3},{2,0},{3,1},{4,6},{5,7},{6,4},{7,5},{8,10},{9,11},{10,... | collective-permute-start | bytes 4718600 | tf_op jit(solution)/shard_map/ppermute | solution.py:23
  237.2 1.6 multiply_add_fusion.2
  238.8 66.3 %collective-permute-done.7 = bf16[96,2,32,128]{3,2,1,0:T(8,128)(2,1)} collective-permute-done((bf16[96,2,32,128]{3,2,1,0:T(8,128)(2,1)}, bf16[96,2,32,128]{3,2,1,0:T(8,128)(2,1)}, u32[]{:S(2)}, u32[]{:S(2)}) %collective-permute-start.7) | collective-permute-done | bytes 1572896 | tf_op jit(solution)/shard_map/ppermute | solution.py:23
  305.2 2.6 fusion.36
  307.7 1.4 fusion.37
  (480 shorter events, 108.0 us)
Async XLA Ops:
  0.0 33.1 %copy-start = (s32[128,6]{0,1:T(8,128)S(1)}, s32[128,6]{0,1:T(8,128)}, u32[]{:S(2)}) copy-start(s32[128,6]{0,1:T(8,128)} %param.9) | copy-start | bytes 9220
  0.0 78.1 %copy-start.4 = (s32[7]{0:T(128)S(1)}, s32[7]{0:T(128)}, u32[]{:S(2)}) copy-start(s32[7]{0:T(128)} %param.11) | copy-start | bytes 88
  0.0 11.8 %collective-permute-start = (bf16[4,16,2,16,128]{4,3,2,1,0:T(8,128)(2,1)}, bf16[4,16,2,16,128]{4,3,2,1,0:T(8,128)(2,1)S(1)}, u32[]{:S(2)}, u32[]{:S(2)}) collective-permute-start(bf16[4,16,2,16,128]{4,3,2,1,0:T(8,128)(2,1)} %param.8), channel_id=1, source_target_pairs={{0,508},{4,0},{8,4},{12,8},{16,12},{20,16},{24,20},{28,24},{32,28}... | collective-permute-start | bytes 1572872 | tf_op jit(solution)/shard_map/ppermute | solution.py:17
  11.8 36.1 %copy-start.2 = (bf16[4,16,2,16,128]{4,3,2,1,0:T(8,128)(2,1)}, bf16[4,16,2,16,128]{4,3,2,1,0:T(8,128)(2,1)S(1)}, u32[]{:S(2)}) copy-start(bf16[4,16,2,16,128]{4,3,2,1,0:T(8,128)(2,1)S(1)} %collective-permute-done) | copy-start | bytes 1572868
  11.8 10.5 %collective-permute-start.1 = (bf16[4,16,2,16,128]{4,3,2,1,0:T(8,128)(2,1)S(1)}, bf16[4,16,2,16,128]{4,3,2,1,0:T(8,128)(2,1)S(1)}, u32[]{:S(2)}, u32[]{:S(2)}) collective-permute-start(bf16[4,16,2,16,128]{4,3,2,1,0:T(8,128)(2,1)S(1)} %collective-permute-done), channel_id=1, source_target_pairs={{0,508},{4,0},{8,4},{12,8},{16,12},{20,16},{24,20},{28,24},{32,28}... | collective-permute-start | bytes 1572872 | tf_op jit(solution)/shard_map/ppermute | solution.py:17
  22.2 25.6 %copy-start.3 = (bf16[4,16,2,16,128]{4,3,2,1,0:T(8,128)(2,1)}, bf16[4,16,2,16,128]{4,3,2,1,0:T(8,128)(2,1)S(1)}, u32[]{:S(2)}) copy-start(bf16[4,16,2,16,128]{4,3,2,1,0:T(8,128)(2,1)S(1)} %collective-permute-done.1) | copy-start | bytes 1572868
  22.2 12.5 %collective-permute-start.2 = (bf16[4,16,2,16,128]{4,3,2,1,0:T(8,128)(2,1)S(1)}, bf16[4,16,2,16,128]{4,3,2,1,0:T(8,128)(2,1)}, u32[]{:S(2)}, u32[]{:S(2)}) collective-permute-start(bf16[4,16,2,16,128]{4,3,2,1,0:T(8,128)(2,1)S(1)} %collective-permute-done.1), channel_id=1, source_target_pairs={{0,508},{4,0},{8,4},{12,8},{16,12},{20,16},{24,20},{28,24},{32,28}... | collective-permute-start | bytes 1572872 | tf_op jit(solution)/shard_map/ppermute | solution.py:17
  34.8 15.2 %collective-permute-start.3 = (bf16[4,16,2,16,128]{4,3,2,1,0:T(8,128)(2,1)}, bf16[4,16,2,16,128]{4,3,2,1,0:T(8,128)(2,1)}, u32[]{:S(2)}, u32[]{:S(2)}) collective-permute-start(bf16[4,16,2,16,128]{4,3,2,1,0:T(8,128)(2,1)} %collective-permute-done.2), channel_id=1, source_target_pairs={{0,508},{4,0},{8,4},{12,8},{16,12},{20,16},{24,20},{28,24},{32,28}... | collective-permute-start | bytes 1572872 | tf_op jit(solution)/shard_map/ppermute | solution.py:17
  50.0 15.8 %collective-permute-start.4 = (bf16[4,16,2,16,128]{4,3,2,1,0:T(8,128)(2,1)}, bf16[4,16,2,16,128]{4,3,2,1,0:T(8,128)(2,1)}, u32[]{:S(2)}, u32[]{:S(2)}) collective-permute-start(bf16[4,16,2,16,128]{4,3,2,1,0:T(8,128)(2,1)} %collective-permute-done.3), channel_id=1, source_target_pairs={{0,508},{4,0},{8,4},{12,8},{16,12},{20,16},{24,20},{28,24},{32,28}... | collective-permute-start | bytes 1572872 | tf_op jit(solution)/shard_map/ppermute | solution.py:17
  65.8 14.1 %collective-permute-start.5 = (bf16[4,16,2,16,128]{4,3,2,1,0:T(8,128)(2,1)}, bf16[4,16,2,16,128]{4,3,2,1,0:T(8,128)(2,1)}, u32[]{:S(2)}, u32[]{:S(2)}) collective-permute-start(bf16[4,16,2,16,128]{4,3,2,1,0:T(8,128)(2,1)} %collective-permute-done.4), channel_id=1, source_target_pairs={{0,508},{4,0},{8,4},{12,8},{16,12},{20,16},{24,20},{28,24},{32,28}... | collective-permute-start | bytes 1572872 | tf_op jit(solution)/shard_map/ppermute | solution.py:17
  79.9 28.9 %collective-permute-start.6 = (bf16[4,16,2,16,128]{4,3,2,1,0:T(8,128)(2,1)}, bf16[4,16,2,16,128]{4,3,2,1,0:T(8,128)(2,1)}, u32[]{:S(2)}, u32[]{:S(2)}) collective-permute-start(bf16[4,16,2,16,128]{4,3,2,1,0:T(8,128)(2,1)} %collective-permute-done.5), channel_id=1, source_target_pairs={{0,508},{4,0},{8,4},{12,8},{16,12},{20,16},{24,20},{28,24},{32,28}... | collective-permute-start | bytes 1572872 | tf_op jit(solution)/shard_map/ppermute | solution.py:17
  226.9 9.5 %copy-start.1 = (s32[512]{0:T(512)S(1)}, s32[512]{0:T(512)}, u32[]{:S(2)}) copy-start(s32[512]{0:T(512)} %param.10) | copy-start | bytes 6148
  228.4 76.7 %collective-permute-start.7 = (bf16[96,2,32,128]{3,2,1,0:T(8,128)(2,1)}, bf16[96,2,32,128]{3,2,1,0:T(8,128)(2,1)}, u32[]{:S(2)}, u32[]{:S(2)}) collective-permute-start(bf16[96,2,32,128]{3,2,1,0:T(8,128)(2,1)} %bitcast_convert_fusion), channel_id=1, source_target_pairs={{0,2},{1,3},{2,0},{3,1},{4,6},{5,7},{6,4},{7,5},{8,10},{9,11},{10,... | collective-permute-start | bytes 4718600 | tf_op jit(solution)/shard_map/ppermute | solution.py:23
where the time goes:
time: 312 us; the launch traced here: 309 us
  waiting for transfers between devices  81.7 us (26%)
  starting transfers between devices  79.7 us (26%)
  local copies, waits for them, and re-layouts  57.6 us (18%)
  matrix products  57.5 us (18%)
  other arithmetic  29.8 us (10%)
    ppermute x7, starting transfers between devices, passed_along(): lax.ppermute(value, axis, [(i, (i + by) % size) for i in range(size)])  71.8 us
    ppermute x1, waiting for transfers between devices, swapped(): return lax.ppermute(value, axis, pairs)  66.3 us
    dot_general x24, matrix products, correlate(): jnp.einsum('nbchk,chdt->nbdtk', banded, section_one, precision=highest)  24.6 us
    dot_general x24, matrix products, correlate(): jnp.einsum('nbdtk,dkeu->nbetu', turned, section_two, precision=highest)  23.9 us
    dynamic_slice x24, local copies, waits for them, and re-layouts, body(): snr_rows, chi_square = lax.map(correlate_with(), templates)  18.3 us
    gather x7, local copies, waits for them, and re-layouts, body(): chosen = place_rows(chosen, moving[local_id], offsets == distance)  18.2 us
    dynamic_update_slice x48, local copies, waits for them, and re-layouts, body(): snr_rows, chi_square = lax.map(correlate_with(), templates)  15.7 us
    ppermute x7, waiting for transfers between devices, passed_along(): lax.ppermute(value, axis, [(i, (i + by) % size) for i in range(size)])  15.4 us
  transfers between devices with their start and end apart: 8, of which 5 were waited for; matrix products, arithmetic and copies ran while one was open for 8% of the time, Pallas kernels for 0%

commit v1 on v0

v1 whole, which is shorter than its diff:
```python
import functools

import jax
import jax.numpy as jnp
import numpy as np
from jax import lax
from jax.experimental import pallas as pl
from jax.experimental.pallas import tpu as pltpu
from jax.sharding import PartitionSpec as P

MESH = pl.DeviceIdType.MESH
EPS = 1e-06
ONE_SCALE = 1.62445
TWO_SCALE = 1.62475
BANDS = 8
ROWS = 592
REACH = 8
UNIT = 4


def tables():
    first = np.zeros((ROWS, 256))
    turn = 2 * np.pi * np.outer(np.arange(32), np.arange(16)) / 32
    cos, sin = np.cos(turn), np.sin(turn)
    from_re, from_im = (cos, sin), (-sin, cos)
    for out_part in range(2):
        both = np.concatenate([from_re[out_part], from_im[out_part]], axis=1)
        for band in range(BANDS):
            at = out_part * 256 + band * 32
            first[at : at + 32, :128] = np.tile(both, (1, 4))
        at = 512 + out_part * 32
        first[at : at + 32, 128:192] = np.tile(both, (1, 2))
    first *= ONE_SCALE
    first[576:584, 192:] = 1.0
    turn = 2 * np.pi * np.outer(np.arange(32), np.arange(128)) / 4096
    twist = np.stack([np.cos(turn), np.sin(turn)]) / (ONE_SCALE * TWO_SCALE)
    turn = 2 * np.pi * (np.outer(np.arange(128), np.arange(128)) % 128) / 128
    cos, sin = np.cos(turn), np.sin(turn)
    second = TWO_SCALE * np.block([[cos, sin], [-sin, cos]])
    return (
        jnp.asarray(first, jnp.bfloat16),
        jnp.asarray(twist, jnp.float32),
        jnp.asarray(second, jnp.bfloat16),
    )


def move_kernel(bank, strain, held, partner, send_sem, recv_sem, own_sem, strain_sem):
    chunks = bank.shape[0]
    segs = lax.axis_size("seg")
    dets = lax.axis_size("det")
    seg = lax.axis_index("seg")
    det = lax.axis_index("det")
    core = lax.rem(seg, 2)
    low = lax.rem(lax.div(seg, 2), 2)
    part = 2 * low + core
    peer = seg + 1 - 2 * core
    across = seg + 2 - 4 * low

    def wrapped(index):
        return lax.rem(index + segs, segs)

    next_det = lax.rem(det + 1, dets)
    prev_det = lax.rem(det + dets - 1, dets)
    other = lax.rem(det + 2, dets) if dets == 4 else det
    barrier = pltpu.get_barrier_semaphore()

    def greet(to_seg, to_det):
        pl.semaphore_signal(barrier, inc=1, device_id=(to_seg, to_det), device_id_type=MESH)

    greet(wrapped(seg + 4), det)
    greet(peer, det)
    greet(across, det)
    greet(seg, other)

    @pl.when(low == 0)
    def _():
        greet(seg + 2, prev_det)

    @pl.when(core == 1)
    def _():
        greet(wrapped(seg + 3), det)

    @pl.when(part == 2)
    def _():
        greet(wrapped(seg + 5), det)

    pl.semaphore_wait(barrier, 4 + low + (1 - core) + jnp.where(part == 3, 1, 0))

    def copy(kind, source, k, slot, to_seg, to_det):
        return pltpu.make_async_remote_copy(
            src_ref=source,
            dst_ref=held.at[slot, k],
            send_sem=send_sem.at[kind, k],
            recv_sem=recv_sem.at[slot, k],
            device_id=(to_seg, to_det),
            device_id_type=MESH,
        )

    def own_along(k):
        return copy(0, bank.at[k], k, 4, wrapped(seg - 4), det)

    def own_peer(k):
        return copy(1, bank.at[k], k, 1, peer, det)

    def own_across(k):
        return copy(2, bank.at[k], k, 2, seg - 2, next_det)

    def pass_two(k):
        return copy(1, held.at[2, k], k, 1 + 2 * core, peer, det)

    def pass_four_peer(k):
        return copy(3, held.at[4, k], k, 3 + 2 * core, peer, det)

    def pass_four_across(k):
        return copy(4, held.at[4, k], k, 2 + 4 * low, across, det)

    def pass_four_along(k):
        return copy(5, held.at[4, k], k, 7, wrapped(seg - 3), det)

    slot_across = 6 - 4 * low

    def pass_across_peer(k):
        return copy(6, held.at[slot_across, k], k, slot_across - 1 + 2 * core, peer, det)

    def pass_across_along(k):
        return copy(5, held.at[2, k], k, 7, wrapped(seg - 5), det)

    def relay_one(k):
        return copy(7, held.at[7, k], k, 5, seg + 2, det)

    def relay_two(k):
        return copy(7, held.at[7, k], k, 6, peer, det)

    def relay_three(k):
        return copy(7, held.at[5, k], k, 6, peer, det)

    def arrived(slot, k):
        pltpu.make_async_copy(held.at[slot, k], held.at[slot, k], recv_sem.at[slot, k]).wait()

    exchange = pltpu.make_async_remote_copy(
        src_ref=strain.at[0, 0],
        dst_ref=partner,
        send_sem=strain_sem.at[0],
        recv_sem=strain_sem.at[1],
        device_id=(seg, other),
        device_id_type=MESH,
    )
    stay = pltpu.make_async_copy(bank, held.at[0], own_sem)
    for k in range(chunks):
        own_along(k).start()

        @pl.when(low == 1)
        def _():
            own_across(k).start()

    for k in range(chunks):

        @pl.when(core == 1)
        def _():
            own_peer(k).start()

    exchange.start()
    stay.start()
    for step in range(chunks + 3):
        k = step
        if k < chunks:
            arrived(4, k)

            @pl.when(core == 0)
            def _():
                pass_four_along(k).start()

            pass_four_across(k).start()
            pass_four_peer(k).start()
        k = step - 1
        if 0 <= k < chunks:
            arrived(slot_across, k)

            @pl.when(part == 3)
            def _():
                pass_across_along(k).start()

            pass_across_peer(k).start()

            @pl.when(low == 0)
            def _():
                arrived(2, k)

            @pl.when(part == 0)
            def _():
                pass_two(k).start()

            @pl.when(part == 1)
            def _():
                own_peer(k).wait_send()
                pass_two(k).start()

        k = step - 2
        if 0 <= k < chunks:

            @pl.when(part == 1)
            def _():
                arrived(7, k)
                relay_one(k).start()

            @pl.when(part == 2)
            def _():
                arrived(7, k)
                relay_two(k).start()

        k = step - 3
        if 0 <= k < chunks:

            @pl.when(part == 3)
            def _():
                arrived(5, k)
                relay_three(k).start()

    for k in range(chunks):
        arrived(1, k)
        arrived(3, k)

        @pl.when(part != 3)
        def _():
            arrived(5, k)

        @pl.when(low == 1)
        def _():
            arrived(6, k)

        @pl.when((part == 0) | (part == 3))
        def _():
            arrived(7, k)

        own_along(k).wait_send()

        @pl.when(low == 1)
        def _():
            own_across(k).wait_send()

        @pl.when((low == 0) | (core == 1))
        def _():
            own_peer(k).wait_send()

        pass_four_peer(k).wait_send()
        pass_four_across(k).wait_send()

        @pl.when((core == 0) | (part == 3))
        def _():
            pass_four_along(k).wait_send()

        pass_across_peer(k).wait_send()

        @pl.when(part != 0)
        def _():
            relay_one(k).wait_send()

    exchange.wait()
    stay.wait()


def move(bank, strain):
    return pl.pallas_call(
        move_kernel,
        out_shape=(
            jax.ShapeDtypeStruct((REACH,) + bank.shape, bank.dtype),
            jax.ShapeDtypeStruct(strain.shape[2:], strain.dtype),
        ),
        in_specs=[pl.BlockSpec(memory_space=pl.ANY)] * 2,
        out_specs=(pl.BlockSpec(memory_space=pl.ANY),) * 2,
        scratch_shapes=[
            pltpu.SemaphoreType.DMA((8, bank.shape[0])),
            pltpu.SemaphoreType.DMA((REACH, bank.shape[0])),
            pltpu.SemaphoreType.DMA,
            pltpu.SemaphoreType.DMA((2,)),
        ],
        compiler_params=pltpu.CompilerParams(
            collective_id=0, has_side_effects=True
        ),
        name="move",
    )(bank, strain)


def band_at(bins, edges):
    return sum(jnp.where(bins >= edges[e], 1, 0) for e in range(BANDS - 1))


def filter_kernel(
    held, strain, partner, bank_list, block_len, edges, first, twist, second, out,
    blocks, banded, cross, stage, turned, result, order, block_sem, out_sem,
):
    segs = lax.axis_size("seg")
    seg = lax.axis_index("seg")
    assign = blocks.shape[0]
    owned = held.shape[1]
    width = blocks.shape[1]
    slots = assign * width

    def fetch(q):
        block = bank_list[q, seg]
        owner = lax.div(block, owned)
        offset = lax.rem(owner - seg + segs, segs)
        return pltpu.make_async_copy(
            held.at[offset, lax.rem(block, owned)], blocks.at[q], block_sem.at[q]
        )

    def give(q):
        rows = pl.ds(q * width, width)
        return pltpu.make_async_copy(result.at[rows], out.at[0, 0, rows], out_sem.at[q])

    for q in range(assign):
        fetch(q).start()

    ends = []
    end = 0
    for q in range(assign):
        live = block_len[bank_list[q, seg]]

        @pl.loop(0, live)
        def _(m, q=q, start=end):
            order[start + m] = q * width + m

        end = end + live
        ends.append(end)

        @pl.loop(live, width)
        def _(m, q=q):
            result[q * width + m] = jnp.zeros(result.shape[1:], jnp.float32)

    for m in range(2 * UNIT):
        order[end + m] = slots

    row = lax.broadcasted_iota(jnp.int32, (ROWS, 256), 0)
    lane = lax.broadcasted_iota(jnp.int32, (1, 256), 1)
    high_lane = jnp.where(lane < 128, lax.rem(lax.div(lane, 32), 2), lax.rem(lax.div(lane, 16), 2))
    lane_band = band_at(lax.rem(lane, 16) * 128 + 127 * high_lane, edges)
    row_band = jnp.where(row < 512, lax.rem(lax.div(row, 32), BANDS), row - 576)
    keep = ((row >= 512) & (row < 576)) | (row_band == lane_band)
    banded[...] = jnp.where(keep, first[...].astype(jnp.float32), 0.0).astype(jnp.bfloat16)

    bins = lax.broadcasted_iota(jnp.int32, (16, 128), 0) * 128
    at_low = band_at(bins, edges)
    at_own = band_at(bins + lax.broadcasted_iota(jnp.int32, (16, 128), 1), edges)
    low_mask = jnp.where(at_low == at_own, 1.0, 0.0)
    high_mask = (1.0 - low_mask).astype(jnp.bfloat16)
    low_mask = low_mask.astype(jnp.bfloat16)

    data_re = strain[0, 0, 0].astype(jnp.float32)
    data_im = strain[0, 0, 1].astype(jnp.float32)
    other_re = partner[0].astype(jnp.float32)
    other_im = partner[1].astype(jnp.float32)

    def halves(value):
        top = value.astype(jnp.bfloat16)
        return top, (value - top.astype(jnp.float32)).astype(jnp.bfloat16)

    def products(unit, h):
        for t in range(2):
            lanes = slice(t * 128, t * 128 + 128)
            slot = order[unit * UNIT + 2 * h + t]
            slot = jnp.where(slot == slots, 0, slot)
            q, m = lax.div(slot, width), lax.rem(slot, width)
            tmpl_re = blocks[q, m, 0].astype(jnp.float32)
            tmpl_im = blocks[q, m, 1].astype(jnp.float32)

            def put(at, value):
                cross[h, at : at + 16, lanes] = value

            for at, value in (
                (0, data_re * tmpl_re + data_im * tmpl_im),
                (16, data_im * tmpl_re - data_re * tmpl_im),
            ):
                top, rest = halves(value)
                put(at, top * low_mask)
                put(at + 32, top * high_mask)
                put(at + 64, rest * low_mask)
                put(at + 96, rest * high_mask)
            for at, value in (
                (128, other_re * tmpl_re + other_im * tmpl_im),
                (144, other_im * tmpl_re - other_re * tmpl_im),
            ):
                top, rest = halves(value)
                put(at, top)
                put(at + 32, rest)
            top, rest = halves(tmpl_re * tmpl_re + tmpl_im * tmpl_im)
            put(192, top * low_mask)
            put(208, top * high_mask)
            put(224, rest * low_mask)
            put(240, rest * high_mask)
        stage[h] = jnp.dot(banded[...], cross[h], preferred_element_type=jnp.float32)

    def turn(h):
        cos, sin = twist[0], twist[1]
        for t in range(2):
            lanes = slice(t * 128, t * 128 + 128)
            for band in range(BANDS + 1):
                at = 512 if band == BANDS else 32 * band
                gap = 32 if band == BANDS else 256
                part_re = stage[h, at : at + 32, lanes]
                part_im = stage[h, at + gap : at + gap + 32, lanes]
                rows = slice(32 * band, 32 * band + 32)
                turned[h, t, rows, :128] = (part_re * cos - part_im * sin).astype(jnp.bfloat16)
                turned[h, t, rows, 128:] = (part_re * sin + part_im * cos).astype(jnp.bfloat16)

    def finish(unit, h, powers):
        for t in range(2):
            power = powers[t]
            total = jnp.sum(power, axis=0, keepdims=True)
            weight = 1.0 / power
            series = jnp.dot(turned[h, t], second[...], preferred_element_type=jnp.float32)
            norm = lax.rsqrt(total)
            sum_re = sum_im = spread = 0.0
            for band in range(BANDS):
                band_re = series[32 * band : 32 * band + 32, :128]
                band_im = series[32 * band : 32 * band + 32, 128:]
                sum_re = sum_re + band_re
                sum_im = sum_im + band_im
                spread = spread + (band_re * band_re + band_im * band_im) * weight[band : band + 1]
            snr_re = sum_re * norm
            snr_im = sum_im * norm
            chi_square = spread - (snr_re * snr_re + snr_im * snr_im)
            join_re = snr_re + series[256:, :128] * norm
            join_im = snr_im + series[256:, 128:] * norm
            coherent = 0.5 * (join_re * join_re + join_im * join_im)
            chi_square = jnp.maximum(chi_square, 0.0)
            result[order[unit * UNIT + 2 * h + t]] = coherent / (
                1.0 + chi_square * (1.0 / (2 * (BANDS - 1)))
            )

    for q in range(assign):
        fetch(q).wait()
    for h in range(UNIT // 2):
        products(0, h)
    done = 0
    for q in range(assign):
        last = q == assign - 1
        upto = lax.div(ends[q] + (UNIT - 1 if last else 0), UNIT)

        @pl.loop(done, upto)
        def _(unit):
            powers = []
            for h in range(UNIT // 2):
                turn(h)
                powers.append(
                    [
                        jnp.sum(stage[h, 576:584, t * 128 : t * 128 + 128], axis=1, keepdims=True) + EPS
                        for t in range(2)
                    ]
                )
            for h in range(UNIT // 2):
                finish(unit, h, powers[h])
                products(unit + 1, h)

        for g in range(q + 1):

            @pl.when((ends[g] <= UNIT * upto) & (ends[g] > UNIT * done) if not last else ends[g] > UNIT * done)
            def _(g=g):
                give(g).start()

        done = upto

    for q in range(assign):
        give(q).wait()


def correlate(held, strain, partner, bank_list, block_len, edges):
    _, owned, width, _, half_rows, bins = held.shape
    assign = bank_list.shape[1]
    slots = assign * width
    vmem = pl.BlockSpec(memory_space=pltpu.VMEM)
    smem = pl.BlockSpec(memory_space=pltpu.SMEM)
    hbm = pl.BlockSpec(memory_space=pl.ANY)
    return pl.pallas_call(
        filter_kernel,
        out_shape=jax.ShapeDtypeStruct((1, 1, slots, 2 * half_rows, bins), jnp.float32),
        in_specs=[hbm, vmem, vmem, smem, smem, smem, vmem, vmem, vmem],
        out_specs=hbm,
        scratch_shapes=[
            pltpu.VMEM((assign,) + held.shape[2:], held.dtype),
            pltpu.VMEM((ROWS, 256), jnp.bfloat16),
            pltpu.VMEM((UNIT // 2, 256, 256), jnp.bfloat16),
            pltpu.VMEM((UNIT // 2, ROWS, 256), jnp.float32),
            pltpu.VMEM((UNIT // 2, 2, 288, 256), jnp.bfloat16),
            pltpu.VMEM((slots + 1, 2 * half_rows, bins), jnp.float32),
            pltpu.SMEM((slots + 2 * UNIT,), jnp.int32),
            pltpu.SemaphoreType.DMA((assign,)),
            pltpu.SemaphoreType.DMA((assign,)),
        ],
        compiler_params=pltpu.CompilerParams(vmem_limit_bytes=60 * 2**20),
        name="filter",
    )(held, strain, partner, bank_list.T, block_len, edges, *tables())


def body(strain, bank, bank_list, block_len, band_edges):
    held, partner = move(bank, strain)
    return correlate(held, strain, partner, bank_list, block_len, band_edges)


def solution(mesh):
    return jax.shard_map(
        body,
        mesh=mesh,
        in_specs=(
            P("det", "seg", None, None, None),
            P("seg", None, None, None, None),
            P(),
            P(),
            P(),
        ),
        out_specs=P("det", "seg", None, None, None),
        check_vma=False,
    )
```

time: 312 us -> 52 us (0.17)
  the two profiles are of different devices: /device:TPU:129 before, /device:TPU:90 now
where the time goes in v1:
time: 52 us; the launch traced here: 51.9 us
  Pallas kernels  51.9 us (100%)
    pallas_call x1, Pallas kernels, move(): pl.pallas_call(move_kernel, out_shape=(jax.ShapeDtypeStruct((REACH,) + ba...  35.6 us
    pallas_call x1, Pallas kernels, correlate(): pl.pallas_call(filter_kernel, out_shape=jax.ShapeDtypeStruct((1, 1, slots...  16.3 us

profile of v1, /device:TPU:90, one launch (start us, length us, event | category | flops | bytes accessed | tf_op | source)
XLA Modules:
  0.0 51.9 jit_solution(10240402321760211705)
XLA Ops:
  0.0 35.6 %move.1 = (bf16[8,4,16,2,16,128]{5,4,3,2,1,0:T(8,128)(2,1)}, bf16[2,16,128]{2,1,0:T(8,128)(2,1)}) custom-call(bf16[4,16,2,16,128]{4,3,2,1,0:T(8,128)(2,1)} %bank.1, bf16[1,1,2,16,128]{4,3,2,1,0:T(8,128)(2,1)} %strain.3), custom_call_target="tpu_custom_call" | custom-call | tf_op jit(solution)/shard_map/move/pallas_call | solution.py:263
  35.6 16.3 %filter.1 = f32[1,1,96,32,128]{4,3,2,1,0:T(8,128)} custom-call(bf16[8,4,16,2,16,128]{5,4,3,2,1,0:T(8,128)(2,1)} %get-tuple-element.7.held, bf16[1,1,2,16,128]{4,3,2,1,0:T(8,128)(2,1)} %strain.3, bf16[2,16,128]{2,1,0:T(8,128)(2,1)} %get-tuple-element.8.partner, s32[6,128]{1,0:T(8,128)} %bitcast.1, s32[512]{0:T(512)} %block_len.1, s32[7]{0:T(128)} %edges.1, ...), custom_call_target="tpu_custom_call" | custom-call | tf_op jit(solution)/shard_map/filter/pallas_call | solution.py:473

commit v2 on v1

--- a/solution.py
+++ b/solution.py
@@ -15,6 +15,8 @@
 BANDS = 8
 ROWS = 592
 REACH = 8
+ALONG = 4
+CHUNKS = 4
 UNIT = 4
 
 
@@ -44,8 +46,11 @@
     )
 
 
-def move_kernel(bank, strain, held, partner, send_sem, recv_sem, own_sem, strain_sem):
+def move_kernel(
+    bank, strain, held, passing, partner, line, send_sem, recv_sem, pass_sem, own_sem, line_sem
+):
     chunks = bank.shape[0]
+    half = chunks // 2
     segs = lax.axis_size("seg")
     dets = lax.axis_size("det")
     seg = lax.axis_index("seg")
@@ -55,13 +60,19 @@
     part = 2 * low + core
     peer = seg + 1 - 2 * core
     across = seg + 2 - 4 * low
+    last = dets - 1
+    around = 4 * ALONG
 
     def wrapped(index):
         return lax.rem(index + segs, segs)
 
+    def beside(index, by):
+        return lax.div(index, around) * around + lax.rem(index + by + around, around)
+
+    above = beside(seg, 4)
+    below = beside(seg, -4)
     next_det = lax.rem(det + 1, dets)
     prev_det = lax.rem(det + dets - 1, dets)
-    other = lax.rem(det + 2, dets) if dets == 4 else det
     barrier = pltpu.get_barrier_semaphore()
 
     def greet(to_seg, to_det):
@@ -70,130 +81,211 @@
     greet(wrapped(seg + 4), det)
     greet(peer, det)
     greet(across, det)
-    greet(seg, other)
 
     @pl.when(low == 0)
     def _():
-        greet(seg + 2, prev_det)
+        greet(across, prev_det)
+
+    @pl.when((low == 1) & (det < last))
+    def _():
+        greet(across, det + 1)
+
+    @pl.when(core == 0)
+    def _():
+        greet(below, det)
 
     @pl.when(core == 1)
     def _():
+        greet(beside(wrapped(seg + 7), 4), det)
+
+    @pl.when(part == 2)
+    def _():
         greet(wrapped(seg + 3), det)
-
-    @pl.when(part == 2)
-    def _():
         greet(wrapped(seg + 5), det)
 
-    pl.semaphore_wait(barrier, 4 + low + (1 - core) + jnp.where(part == 3, 1, 0))
+    pl.semaphore_wait(barrier, 5 - core + jnp.where((low == 1) | (det > 0), 1, 0))
 
     def copy(kind, source, k, slot, to_seg, to_det):
         return pltpu.make_async_remote_copy(
             src_ref=source,
             dst_ref=held.at[slot, k],
-            send_sem=send_sem.at[kind, k],
-            recv_sem=recv_sem.at[slot, k],
+            send_sem=send_sem.at[kind],
+            recv_sem=recv_sem.at[slot, jnp.where((slot == 1) | (slot == 3), 0, k)],
             device_id=(to_seg, to_det),
             device_id_type=MESH,
         )
 
-    def own_along(k):
-        return copy(0, bank.at[k], k, 4, wrapped(seg - 4), det)
-
-    def own_peer(k):
-        return copy(1, bank.at[k], k, 1, peer, det)
-
-    def own_across(k):
-        return copy(2, bank.at[k], k, 2, seg - 2, next_det)
-
-    def pass_two(k):
-        return copy(1, held.at[2, k], k, 1 + 2 * core, peer, det)
-
-    def pass_four_peer(k):
-        return copy(3, held.at[4, k], k, 3 + 2 * core, peer, det)
-
-    def pass_four_across(k):
-        return copy(4, held.at[4, k], k, 2 + 4 * low, across, det)
-
-    def pass_four_along(k):
-        return copy(5, held.at[4, k], k, 7, wrapped(seg - 3), det)
-
-    slot_across = 6 - 4 * low
-
-    def pass_across_peer(k):
-        return copy(6, held.at[slot_across, k], k, slot_across - 1 + 2 * core, peer, det)
-
-    def pass_across_along(k):
-        return copy(5, held.at[2, k], k, 7, wrapped(seg - 5), det)
-
-    def relay_one(k):
-        return copy(7, held.at[7, k], k, 5, seg + 2, det)
-
-    def relay_two(k):
-        return copy(7, held.at[7, k], k, 6, peer, det)
-
-    def relay_three(k):
-        return copy(7, held.at[5, k], k, 6, peer, det)
-
     def arrived(slot, k):
         pltpu.make_async_copy(held.at[slot, k], held.at[slot, k], recv_sem.at[slot, k]).wait()
 
-    exchange = pltpu.make_async_remote_copy(
-        src_ref=strain.at[0, 0],
-        dst_ref=partner,
-        send_sem=strain_sem.at[0],
-        recv_sem=strain_sem.at[1],
-        device_id=(seg, other),
-        device_id_type=MESH,
-    )
+    def all_arrived(slot):
+        pltpu.make_async_copy(held.at[slot], held.at[slot], recv_sem.at[slot, 0]).wait()
+
+    def sent(kind, count):
+        some = bank.at[pl.ds(0, count)]
+        pltpu.make_async_copy(some, some, send_sem.at[kind]).wait()
+
+    def up_across(kind, source, k, slot):
+        if k % 2 == 0:
+            copy(kind, source, k, slot, seg + 2, det).start()
+        else:
+
+            @pl.when(det > 0)
+            def _():
+                copy(kind, source, k, slot, seg + 2, det - 1).start()
+
+            @pl.when(det == last)
+            def _():
+                copy(kind, source, k, slot, seg + 2, det).start()
+
+    def sent_up_across(kind):
+        sent(kind, half)
+
+        @pl.when(det > 0)
+        def _():
+            sent(kind, half)
+
+        @pl.when(det == last)
+        def _():
+            sent(kind, half)
+
+    def own_along(k):
+        copy(0, bank.at[k], k, 4, wrapped(seg - 4), det).start()
+
+    def own_peer(k):
+        copy(1, bank.at[k], k, 1, peer, det).start()
+
+    def own_across(k):
+        if k % 2 == 0:
+
+            @pl.when(det < last)
+            def _():
+                copy(2, bank.at[k], k, 2, seg - 2, det + 1).start()
+
+            @pl.when(det == 0)
+            def _():
+                copy(2, bank.at[k], k, 2, seg - 2, det).start()
+        else:
+            copy(2, bank.at[k], k, 2, seg - 2, next_det).start()
+
+    def own_above(k):
+        pltpu.make_async_remote_copy(
+            src_ref=bank.at[k],
+            dst_ref=passing.at[k],
+            send_sem=send_sem.at[3],
+            recv_sem=pass_sem.at[k],
+            device_id=(above, det),
+            device_id_type=MESH,
+        ).start()
+
+    def pass_above(k):
+        pltpu.make_async_copy(passing.at[k], passing.at[k], pass_sem.at[k]).wait()
+        copy(4, passing.at[k], k, 7, wrapped(below - 7), det).start()
+
+    def pass_two(k):
+        copy(5, held.at[2, k], k, 1 + 2 * core, peer, det).start()
+
+    def pass_four_peer(k):
+        copy(6, held.at[4, k], k, 3 + 2 * core, peer, det).start()
+
+    def pass_four_across(k):
+        @pl.when(low == 0)
+        def _():
+            up_across(7, held.at[4, k], k, 2)
+
+        @pl.when(low == 1)
+        def _():
+            copy(7, held.at[4, k], k, 6, seg - 2, det).start()
+
+    slot_across = 6 - 4 * low
+
+    def pass_across_peer(k):
+        copy(8, held.at[slot_across, k], k, slot_across - 1 + 2 * core, peer, det).start()
+
     stay = pltpu.make_async_copy(bank, held.at[0], own_sem)
+    height = 2 * det + low
+    hops = dets
+
+    def along_line(way, hop):
+        if way == 0:
+            to_det = det + low
+        else:
+            to_det = det - 1 + low
+        return pltpu.make_async_remote_copy(
+            src_ref=strain.at[0, 0] if hop == 0 else line.at[way, hop - 1],
+            dst_ref=partner if hop == hops - 1 else line.at[way, hop],
+            send_sem=line_sem.at[0, way, hop],
+            recv_sem=line_sem.at[1, way, hop],
+            device_id=(across, to_det),
+            device_id_type=MESH,
+        )
+
+    def on_line(way, hop):
+        origin = height - hop if way == 0 else height + hop
+        return (origin >= way * hops) & (origin < way * hops + hops)
+
+    def pass_line(hop):
+        for way in range(2):
+
+            @pl.when(on_line(way, hop))
+            def _(way=way):
+                if hop > 0:
+                    along_line(way, hop - 1).wait_recv()
+                if hop < hops:
+                    along_line(way, hop).start()
+
     for k in range(chunks):
-        own_along(k).start()
+        own_along(k)
+
+        @pl.when(core == 0)
+        def _():
+            own_above(k)
 
         @pl.when(low == 1)
         def _():
-            own_across(k).start()
-
-    for k in range(chunks):
-
-        @pl.when(core == 1)
-        def _():
-            own_peer(k).start()
-
-    exchange.start()
+            own_across(k)
+
+    @pl.when(core == 1)
+    def _():
+        for k in range(chunks):
+            own_peer(k)
+
+    pass_line(0)
     stay.start()
     for step in range(chunks + 3):
         k = step
         if k < chunks:
+
+            @pl.when(core == 0)
+            def _():
+                pass_above(k)
+
             arrived(4, k)
-
-            @pl.when(core == 0)
-            def _():
-                pass_four_along(k).start()
-
-            pass_four_across(k).start()
-            pass_four_peer(k).start()
+            if k % 2 == 0:
+
+                @pl.when(part == 1)
+                def _():
+                    copy(9, held.at[4, k], k, 7, wrapped(seg - 3), det).start()
+
+            pass_four_across(k)
+            pass_four_peer(k)
+        if 1 <= step <= hops:
+            pass_line(step)
         k = step - 1
         if 0 <= k < chunks:
             arrived(slot_across, k)
-
-            @pl.when(part == 3)
-            def _():
-                pass_across_along(k).start()
-
-            pass_across_peer(k).start()
+            if k % 2 == 1:
+
+                @pl.when(part == 3)
+                def _():
+                    copy(9, held.at[2, k], k, 7, wrapped(seg - 5), det).start()
+
+            pass_across_peer(k)
 
             @pl.when(low == 0)
             def _():
                 arrived(2, k)
-
-            @pl.when(part == 0)
-            def _():
-                pass_two(k).start()
-
-            @pl.when(part == 1)
-            def _():
-                own_peer(k).wait_send()
-                pass_two(k).start()
+                pass_two(k)
 
         k = step - 2
         if 0 <= k < chunks:
@@ -201,12 +293,12 @@
             @pl.when(part == 1)
             def _():
                 arrived(7, k)
-                relay_one(k).start()
+                up_across(10, held.at[7, k], k, 5)
 
             @pl.when(part == 2)
             def _():
                 arrived(7, k)
-                relay_two(k).start()
+                copy(10, held.at[7, k], k, 6, peer, det).start()
 
         k = step - 3
         if 0 <= k < chunks:
@@ -214,11 +306,55 @@
             @pl.when(part == 3)
             def _():
                 arrived(5, k)
-                relay_three(k).start()
-
+                copy(10, held.at[5, k], k, 6, peer, det).start()
+
+    for hop in range(hops):
+        for way in range(2):
+
+            @pl.when(on_line(way, hop))
+            def _(way=way, hop=hop):
+                along_line(way, hop).wait_send()
+
+    sent(0, chunks)
+    sent(6, chunks)
+    sent(8, chunks)
+
+    @pl.when(core == 0)
+    def _():
+        sent(3, chunks)
+        sent(4, chunks)
+
+    @pl.when(core == 1)
+    def _():
+        sent(1, chunks)
+        sent(9, half)
+
+    @pl.when(low == 0)
+    def _():
+        sent(5, chunks)
+        sent_up_across(7)
+
+    @pl.when(low == 1)
+    def _():
+        sent(7, chunks)
+        sent(2, half)
+        sent(10, chunks)
+
+        @pl.when(det < last)
+        def _():
+            sent(2, half)
+
+        @pl.when(det == 0)
+        def _():
+            sent(2, half)
+
+    @pl.when(part == 1)
+    def _():
+        sent_up_across(10)
+
+    all_arrived(1)
+    all_arrived(3)
     for k in range(chunks):
-        arrived(1, k)
-        arrived(3, k)
 
         @pl.when(part != 3)
         def _():
@@ -232,53 +368,34 @@
         def _():
             arrived(7, k)
 
-        own_along(k).wait_send()
-
-        @pl.when(low == 1)
-        def _():
-            own_across(k).wait_send()
-
-        @pl.when((low == 0) | (core == 1))
-        def _():
-            own_peer(k).wait_send()
-
-        pass_four_peer(k).wait_send()
-        pass_four_across(k).wait_send()
-
-        @pl.when((core == 0) | (part == 3))
-        def _():
-            pass_four_along(k).wait_send()
-
-        pass_across_peer(k).wait_send()
-
-        @pl.when(part != 0)
-        def _():
-            relay_one(k).wait_send()
-
-    exchange.wait()
     stay.wait()
 
 
-def move(bank, strain):
-    return pl.pallas_call(
+def move(bank, strain, dets):
+    owned, width = bank.shape[:2]
+    spectrum = strain.shape[2:]
+    bank = bank.reshape((CHUNKS, owned * width // CHUNKS) + bank.shape[2:])
+    held, _, partner, _ = pl.pallas_call(
         move_kernel,
         out_shape=(
             jax.ShapeDtypeStruct((REACH,) + bank.shape, bank.dtype),
-            jax.ShapeDtypeStruct(strain.shape[2:], strain.dtype),
+            jax.ShapeDtypeStruct(bank.shape, bank.dtype),
+            jax.ShapeDtypeStruct(spectrum, strain.dtype),
+            jax.ShapeDtypeStruct((2, dets - 1) + spectrum, strain.dtype),
         ),
         in_specs=[pl.BlockSpec(memory_space=pl.ANY)] * 2,
-        out_specs=(pl.BlockSpec(memory_space=pl.ANY),) * 2,
+        out_specs=(pl.BlockSpec(memory_space=pl.ANY),) * 4,
         scratch_shapes=[
-            pltpu.SemaphoreType.DMA((8, bank.shape[0])),
-            pltpu.SemaphoreType.DMA((REACH, bank.shape[0])),
+            pltpu.SemaphoreType.DMA((11,)),
+            pltpu.SemaphoreType.DMA((REACH, CHUNKS)),
+            pltpu.SemaphoreType.DMA((CHUNKS,)),
             pltpu.SemaphoreType.DMA,
-            pltpu.SemaphoreType.DMA((2,)),
+            pltpu.SemaphoreType.DMA((2, 2, dets)),
         ],
-        compiler_params=pltpu.CompilerParams(
-            collective_id=0, has_side_effects=True
-        ),
+        compiler_params=pltpu.CompilerParams(collective_id=0, has_side_effects=True),
         name="move",
     )(bank, strain)
+    return held.reshape((REACH, owned, width) + bank.shape[2:]), partner
 
 
 def band_at(bins, edges):
@@ -403,11 +520,14 @@
                 turned[h, t, rows, 128:] = (part_re * sin + part_im * cos).astype(jnp.bfloat16)
 
     def finish(unit, h, powers):
+        both = jnp.dot(
+            turned[h].reshape(576, 256), second[...], preferred_element_type=jnp.float32
+        )
         for t in range(2):
             power = powers[t]
             total = jnp.sum(power, axis=0, keepdims=True)
             weight = 1.0 / power
-            series = jnp.dot(turned[h, t], second[...], preferred_element_type=jnp.float32)
+            series = both[288 * t : 288 * t + 288]
             norm = lax.rsqrt(total)
             sum_re = sum_im = spread = 0.0
             for band in range(BANDS):
@@ -492,7 +612,7 @@
 
 
 def body(strain, bank, bank_list, block_len, band_edges):
-    held, partner = move(bank, strain)
+    held, partner = move(bank, strain, lax.axis_size("det"))
     return correlate(held, strain, partner, bank_list, block_len, band_edges)
 
 

time: 52 us -> 47.4 us (0.912)
  the two profiles are of different devices: /device:TPU:90 before, /device:TPU:104 now
where the time goes in v2:
time: 47.4 us; the launch traced here: 47.3 us
  Pallas kernels  47.3 us (100%)
    pallas_call x1, Pallas kernels, move(): pl.pallas_call(move_kernel, out_shape=(jax.ShapeDtypeStruct((REACH,) + ba...  33.4 us
    pallas_call x1, Pallas kernels, correlate(): pl.pallas_call(filter_kernel, out_shape=jax.ShapeDtypeStruct((1, 1, slots...  13.8 us

profile of v2, /device:TPU:104, one launch (start us, length us, event | category | flops | bytes accessed | tf_op | source)
XLA Modules:
  0.0 47.3 jit_solution(6760546080379660622)
XLA Ops:
  0.0 33.4 %move.1 = (bf16[8,4,16,2,16,128]{5,4,3,2,1,0:T(8,128)(2,1)}, bf16[4,16,2,16,128]{4,3,2,1,0:T(8,128)(2,1)}, bf16[2,16,128]{2,1,0:T(8,128)(2,1)}, bf16[2,3,2,16,128]{4,3,2,1,0:T(8,128)(2,1)}) custom-call(bf16[4,16,2,16,128]{4,3,2,1,0:T(8,128)(2,1)} %bank.1, bf16[1,1,2,16,128]{4,3,2,1,0:T(8,128)(2,1)} %strain.3), custom_call_target="tpu_custom_call" | custom-call | tf_op jit(solution)/shard_map/move/pallas_call | solution.py:378
  33.4 13.8 %filter.1 = f32[1,1,96,32,128]{4,3,2,1,0:T(8,128)} custom-call(bf16[8,4,16,2,16,128]{5,4,3,2,1,0:T(8,128)(2,1)} %get-tuple-element.7.held, bf16[1,1,2,16,128]{4,3,2,1,0:T(8,128)(2,1)} %strain.3, bf16[2,16,128]{2,1,0:T(8,128)(2,1)} %get-tuple-element.8.partner, s32[6,128]{1,0:T(8,128)} %bitcast.1, s32[512]{0:T(512)} %block_len.1, s32[7]{0:T(128)} %edges.1, ...), custom_call_target="tpu_custom_call" | custom-call | tf_op jit(solution)/shard_map/filter/pallas_call | solution.py:593
